TPU v7x, 128 devices: a whole 4x4x4 slice. The times are simulated.
128 devices in a mesh: seq: 32 (over y, x_lo, z), batch: 4 (over x_hi, core).
Axes of the slice: x: 4 (x_hi: 2, x_lo: 2; x = x_hi * 2 + x_lo), y: 4, z: 4, core: 2. Of those that a mesh axis runs over, the one named last changes fastest.
Arguments:
- stream: bfloat16 [229376, 1280], P(('batch', 'seq')), parts along dimension 0, may hold values from -6 to 6
- bases: int32 [229376], P(('batch', 'seq')), parts along dimension 0, may hold values from 0 to 4
- input_weight: bfloat16 [2, 1280, 640], replicated, may hold values from -0.15625 to 0.15625
- kernel: bfloat16 [2, 5, 640, 640], replicated, may hold values from -0.109375 to 0.109375
- output_weight: bfloat16 [2, 640, 1280], replicated, may hold values from -0.25 to 0.25
Outputs:
- result: bfloat16 [229376, 1280], P(('batch', 'seq')), parts along dimension 0
There are 4 independent parts, one for each index of `batch`. A program takes and returns all parts, laid end to end along the dimension named above; an argument that names none is the same for every part. Nothing has to cross between parts.
Inputs may be any that keep to these rules, and one draw needn't show every extreme that they name: `bases`: id 4 marks an unknown base, 0 to 3 the four nucleotides.
All inputs are finite; a program needn't handle non-finite values.
Results may differ from a plain program's by a relative error of at most 0.0085.
Values may be sent and summed in bfloat16 or wider, within the bound.
A program may use at most 128 MiB of HBM per device.

v0:
```python
import jax
import jax.numpy as jnp
from jax import lax
from jax.experimental import pallas as pl
from jax.experimental.pallas import tpu as pltpu
from jax.sharding import PartitionSpec as P

D, H, TAPS = 1280, 640, 5
PITCH = 896
FRONT, BIG, BACK = 1, 6, 1
CHUNKS = FRONT + BIG + BACK
BF, F32 = jnp.bfloat16, jnp.float32
VMEM_LIMIT = 54 * 2**20


def gelu_of_norm(v, mask=None):
    centre = v - jnp.mean(v, axis=-1, keepdims=True)
    scale = lax.rsqrt(jnp.mean(centre * centre, axis=-1, keepdims=True) + 1e-05)
    if mask is not None:
        scale = scale * mask
    u = centre * scale
    half = 0.5 * u
    bent = u * (0.7978845608028654 + 0.035677408136300125 * (u * u))
    return (half + half * jnp.tanh(bent)).astype(BF)


def dot(a, b):
    return jnp.dot(a, b, preferred_element_type=F32)


class Chunks:
    def __init__(self, q, count, refs):
        self.q, self.count = q, count
        self.rows, self.half = 8 * q, 4 * q
        if refs is None:
            return
        (
            self.sbuf, self.resid, self.pres, self.s1, self.x1, self.s2, self.a1, self.x2,
            self.load_sem, self.out_sem, self.a_s, self.a_r, self.h_s, self.h_r,
            self.b_s, self.b_r, self.y_s, self.y_r,
        ) = refs

    def scratch(self):
        q, n = self.q, self.count
        dma = pltpu.SemaphoreType.DMA
        plain = pltpu.VMEM((n, self.rows, H), BF)
        return [
            pltpu.VMEM((n, 4, 2, q, D), BF),
            pltpu.VMEM((n, self.rows, D), F32),
            pltpu.VMEM((n, 4, 2, q, 1), F32),
            plain,
            pltpu.VMEM((n, 12 * q, H), BF),
            plain,
            plain,
            pltpu.VMEM((n, 6 * self.half, H), BF),
            dma((n, 2, 4)),
            dma((n, 2, 4)),
            dma((n, 3)),
            dma((n, 3)),
            dma((n, 2)),
            dma((n, 2)),
            dma((n, 3)),
            dma((n, 3)),
            dma((n, 4)),
            dma((n, 4)),
        ]


SETS = ((16, FRONT + BACK), (32, BIG))
FIELDS = 18


def rows(start, size):
    return pl.ds(pl.multiple_of(start, 16), size)


def kernel(x_hbm, bases, win_hbm, kern_hbm, wout_hbm, out_hbm, win, kern, wout, w_sem, *refs):
    small = Chunks(*SETS[0], refs[:FIELDS])
    big = Chunks(*SETS[1], refs[FIELDS:])
    s = lax.axis_index("seq")
    y, g, z = s // 8, s // 4, s % 4
    low = y % 2
    upper = y // 2
    own_v = low + upper - 2 * low * upper
    partner = s + 8 - 16 * low
    cross = (3 - y) * 8 + s % 8
    base = s - z

    def remote(src, dst, send, recv, dev):
        return pltpu.make_async_remote_copy(
            src_ref=src, dst_ref=dst, send_sem=send, recv_sem=recv,
            device_id={"seq": dev}, device_id_type=pl.DeviceIdType.MESH,
        )

    def peer(k):
        return (z + k) % 4

    def gather(m, c, k):
        p, n = peer(k), 2 * m.q
        return remote(
            m.s1.at[c, rows(p * n, n)], m.x1.at[c, rows((1 + z) * n, n)],
            m.a_s.at[c, k - 1], m.a_r.at[c, k - 1], base + p,
        )

    def back(m, c, k):
        p, n = peer(k), 2 * m.q
        return remote(
            m.s2.at[c, rows(p * n, n)], m.a1.at[c, rows(z * n, n)],
            m.b_s.at[c, k - 1], m.b_r.at[c, k - 1], base + p,
        )

    def halo_up(m, c):
        n = 2 * m.q
        return remote(
            m.x1.at[c, pl.ds(4 * n, n)], m.x1.at[c, pl.ds(0, n)],
            m.h_s.at[c, 0], m.h_r.at[c, 0], s + 4,
        )

    def halo_down(m, c):
        n = 2 * m.q
        return remote(
            m.x1.at[c, pl.ds(n, n)], m.x1.at[c, pl.ds(5 * n, n)],
            m.h_s.at[c, 1], m.h_r.at[c, 1], s - 4,
        )

    def to_partner(m, c):
        return remote(
            m.s2.at[c, rows(own_v * m.half, m.half)], m.x2.at[c, rows((y + 1) * m.half, m.half)],
            m.y_s.at[c, 0], m.y_r.at[c, 0], partner,
        )

    def to_cross(m, c):
        return remote(
            m.s2.at[c, rows((1 - own_v) * m.half, m.half)], m.x2.at[c, rows((y + 1) * m.half, m.half)],
            m.y_s.at[c, 1], m.y_r.at[c, 1], cross,
        )

    def relay(m, c):
        part = m.x2.at[c, rows((y + 2 - 2 * low) * m.half, m.half)]
        return remote(part, part, m.y_s.at[c, 2], m.y_r.at[c, 2], cross)

    def to_home(m, c):
        return remote(
            m.s1.at[c, rows((1 - low) * m.half, m.half)], m.a1.at[c, rows((1 - own_v) * m.half, m.half)],
            m.y_s.at[c, 3], m.y_r.at[c, 3], partner,
        )

    def moves(m, c, hbm, sem, store):
        copies = []
        for h in range(2):
            if m is big:
                there, here = hbm.at[h, pl.ds(2 * FRONT + 4 * c, 4)], m.sbuf.at[c, :, h]
                pairs = [(there, here)]
            else:
                first = c * 2 if c < FRONT else 2 * c + 4 * BIG
                pairs = [
                    (hbm.at[h, first + i // 2, pl.ds(16 * (i % 2), 16)], m.sbuf.at[c, i, h])
                    for i in range(4)
                ]
            for i, (there, here) in enumerate(pairs):
                ends = (here, there) if store else (there, here)
                copies.append(pltpu.make_async_copy(*ends, sem.at[c, h, i]))
        return copies

    def loads(m, c):
        return moves(m, c, x_hbm, m.load_sem, False)

    def stores(m, c):
        return moves(m, c, out_hbm, m.out_sem, True)

    weights = {
        "in0": pltpu.make_async_copy(win_hbm.at[0], win.at[0], w_sem.at[0]),
        "k0": pltpu.make_async_copy(kern_hbm.at[0], kern.at[0], w_sem.at[1]),
        "out0": pltpu.make_async_copy(wout_hbm.at[0], wout.at[0], w_sem.at[2]),
        "in1": pltpu.make_async_copy(win_hbm.at[1], win.at[1], w_sem.at[3]),
        "k1": pltpu.make_async_copy(kern_hbm.at[1], kern.at[1], w_sem.at[4]),
        "out1": pltpu.make_async_copy(wout_hbm.at[1], wout.at[1], w_sem.at[5]),
    }

    def first(m, c, *names):
        if m is small and c == 0:
            for name in names:
                weights[name].wait()

    def lower_first(m, c):
        for copy in loads(m, c):
            copy.wait()
        first(m, c, "in0")
        v = m.sbuf[c].reshape(m.rows, D).astype(F32)
        lowered = dot(gelu_of_norm(v), win[0])
        m.s1[c] = gelu_of_norm(lowered, m.pres[c].reshape(m.rows, 1))
        if m is small and c == 0:
            pl.semaphore_wait(barrier, 5 + (g + 6) // 7 + (13 - g) // 7)
        for k in (2, 1, 3):
            gather(m, c, k).start()
        n = 2 * m.q
        m.x1[c, rows((1 + z) * n, n)] = m.s1[c, rows(z * n, n)]

    def send_halo(m, c):
        for k in (1, 2, 3):
            gather(m, c, k).wait_recv()
        pl.when(g < 7)(lambda: halo_up(m, c).start())
        pl.when(g > 0)(lambda: halo_down(m, c).start())

    def near(m, c):
        first(m, c, "k0")
        pl.when(g > 0)(lambda: halo_up(m, c).wait_recv())
        pl.when(g < 7)(lambda: halo_down(m, c).wait_recv())
        wide = jnp.concatenate([m.x1[c, pl.ds(k * m.q, 8 * m.q)] for k in range(TAPS)], axis=1)
        m.s2[c] = gelu_of_norm(dot(wide, kern[0]))
        for k in (2, 1, 3):
            back(m, c, k).start()
        n = 2 * m.q
        m.a1[c, rows(z * n, n)] = m.s2[c, rows(z * n, n)]

    def middle(m, c):
        first(m, c, "out0", "in1")
        for k in (1, 2, 3):
            back(m, c, k).wait_recv()
        m.resid[c] = m.sbuf[c].reshape(m.rows, D).astype(F32) + dot(m.a1[c], wout[0])
        lowered = dot(gelu_of_norm(m.resid[c]), win[1])
        for k in (1, 2, 3):
            back(m, c, k).wait_send()
        m.s2[c] = gelu_of_norm(lowered, m.pres[c].reshape(m.rows, 1))
        to_partner(m, c).start()
        to_cross(m, c).start()
        m.x2[c, rows((y + 1) * m.half, m.half)] = m.s2[c, rows((1 - own_v) * m.half, m.half)]

    def pass_on(m, c):
        to_partner(m, c).wait_recv()
        relay(m, c).start()

    def far(m, c):
        first(m, c, "k1")
        to_cross(m, c).wait_recv()
        relay(m, c).wait_recv()
        for k in (1, 2, 3):
            gather(m, c, k).wait_send()
        wide = jnp.concatenate(
            [m.x2[c, rows((upper + k) * m.half, m.rows)] for k in range(4)], axis=1
        )
        m.s1[c] = gelu_of_norm(dot(wide, kern[1, rows((1 - upper) * H, 4 * H)]))
        to_home(m, c).start()
        m.a1[c, rows((1 - own_v) * m.half, m.half)] = m.s1[c, rows(low * m.half, m.half)]

    def finish(m, c):
        first(m, c, "out1")
        to_home(m, c).wait_recv()
        result = m.resid[c] + dot(m.a1[c], wout[1])
        m.sbuf[c] = result.astype(BF).reshape(4, 2, m.q, D)
        for copy in stores(m, c):
            copy.start()

    barrier = pltpu.get_barrier_semaphore()

    def greet(dev):
        pl.semaphore_signal(barrier, inc=1, device_id={"seq": dev}, device_id_type=pl.DeviceIdType.MESH)

    for k in (1, 2, 3):
        greet(base + peer(k))
    greet(partner)
    greet(cross)
    pl.when(g < 7)(lambda: greet(s + 4))
    pl.when(g > 0)(lambda: greet(s - 4))

    order = [(small, c) for c in range(FRONT)]
    order += [(big, c) for c in range(BIG)]
    order += [(small, c) for c in range(FRONT, FRONT + BACK)]
    for i, (m, c) in enumerate(order):
        for copy in loads(m, c):
            copy.start()
        if i == 0:
            weights["in0"].start()
        if i == 1:
            weights["k0"].start()
        if i == 2:
            weights["out0"].start()
            weights["in1"].start()
    weights["k1"].start()
    weights["out1"].start()

    known = (bases[...] != 4).astype(F32).T
    for c, (m, i) in enumerate(order):
        n = 4 * m.q
        start = 64 * c if c <= FRONT else 64 * FRONT + 128 * (c - FRONT)
        if c > FRONT + BIG:
            start = 64 * (c - BIG) + 128 * BIG
        for h in range(2):
            for j in range(4):
                at = start + j * m.q
                col = h * 7 + at // 128
                m.pres[i, j, h] = known[at % 128 : at % 128 + m.q, col : col + 1]

    for m in (small, big):

        def clear(c, carry):
            m.x2[c, pl.ds(0, m.half)] = jnp.zeros((m.half, H), BF)
            m.x2[c, pl.ds(5 * m.half, m.half)] = jnp.zeros((m.half, H), BF)

            @pl.when(g == 0)
            def _():
                m.x1[c, pl.ds(0, 2 * m.q)] = jnp.zeros((2 * m.q, H), BF)

            @pl.when(g == 7)
            def _():
                m.x1[c, pl.ds(10 * m.q, 2 * m.q)] = jnp.zeros((2 * m.q, H), BF)

            return carry

        lax.fori_loop(0, m.count, clear, 0)

    lower_first(small, 0)

    def at(p, stage):
        for c in range(int(stage is lower_first), FRONT + BACK):
            pl.when(p == (c if c < FRONT else c + BIG))(lambda c=c: stage(small, c))
        pl.when(jnp.logical_and(p >= FRONT, p < FRONT + BIG))(lambda: stage(big, p - FRONT))

    PLAN = [
        (near, 3), (pass_on, 5), (middle, 4), (far, 6),
        (lower_first, 0), (finish, 7), (send_halo, 1),
    ]

    def step(t, carry):
        for stage, lag in PLAN:
            at(t - lag, stage)
        return carry

    lax.fori_loop(0, CHUNKS + max(lag for _, lag in PLAN), step, 0)

    for m in (small, big):

        def drain(m, c):
            pl.when(g < 7)(lambda: halo_up(m, c).wait_send())
            pl.when(g > 0)(lambda: halo_down(m, c).wait_send())
            to_partner(m, c).wait_send()
            to_cross(m, c).wait_send()
            relay(m, c).wait_send()
            to_home(m, c).wait_send()
            for copy in stores(m, c):
                copy.wait()

        for c in range(m.count):
            drain(m, c)


def body(stream, bases, input_weight, kernel_weight, output_weight):
    hbm = pl.BlockSpec(memory_space=pl.ANY)
    vmem = pl.BlockSpec(memory_space=pltpu.VMEM)
    shape = (2, PITCH // 32, 32, D)
    result = pl.pallas_call(
        kernel,
        out_shape=jax.ShapeDtypeStruct(shape, BF),
        in_specs=[hbm, vmem, hbm, hbm, hbm],
        out_specs=hbm,
        scratch_shapes=[
            pltpu.VMEM((2, D, H), BF),
            pltpu.VMEM((2, TAPS * H, H), BF),
            pltpu.VMEM((2, H, D), BF),
            pltpu.SemaphoreType.DMA((6,)),
            *[ref for q, count in SETS for ref in Chunks(q, count, None).scratch()],
        ],
        compiler_params=pltpu.CompilerParams(
            collective_id=0, has_side_effects=True, vmem_limit_bytes=VMEM_LIMIT
        ),
    )(
        stream.reshape(shape),
        bases.reshape(14, 128),
        input_weight,
        kernel_weight.reshape(2, TAPS * H, H),
        output_weight,
    )
    return result.reshape(2 * PITCH, D)


def solution(mesh):
    return jax.shard_map(
        body,
        mesh=mesh,
        in_specs=(P(("batch", "seq"), None), P(("batch", "seq")), P(), P(), P()),
        out_specs=P(("batch", "seq"), None),
        check_vma=False,
    )
```

profile of v0, /device:TPU:2, one launch (start us, length us, event | category | flops | bytes accessed | tf_op | source)
XLA Modules:
  0.0 99.1 jit_solution(9378985364841364604)
XLA Ops:
  0.0 94.4 %shard_map.55 = bf16[2,28,32,1280]{3,2,1,0:T(8,128)(2,1)} custom-call(bf16[2,28,32,1280]{3,2,1,0:T(8,128)(2,1)} %bitcast.6, s32[14,128]{1,0:T(8,128)} %bitcast.7, bf16[2,1280,640]{2,1,0:T(8,128)(2,1)} %win_hbm.1, bf16[2,3200,640]{2,1,0:T(8,128)(2,1)} %bitcast.5, bf16[2,640,1280]{2,1,0:T(8,128)(2,1)} %wout_hbm.1), custom_call_target="tpu_custom_call" | custom-call | tf_op jit(solution)/shard_map/pallas_call | solution.py:351
  94.4 4.7 %copy.7 = bf16[1792,1280]{1,0:T(8,128)(2,1)} copy(bf16[1792,1280]{1,0:T(8,128)(2,1)} %bitcast.4) | data formatting | bytes 9175040
where the time goes:
time: 99.9 us; the launch traced here: 99.1 us
  Pallas kernels  94.4 us (94%)
  local copies, waits for them, and re-layouts  4.74 us (5%)
    pallas_call x1, Pallas kernels, body(): pl.pallas_call(kernel, out_shape=jax.ShapeDtypeStruct(shape, BF), in_spec...  94.4 us
    unnamed x1, local copies, waits for them, and re-layouts  4.74 us

commit v1 on v0

--- a/solution.py
+++ b/solution.py
@@ -36,7 +36,7 @@
             return
         (
             self.sbuf, self.resid, self.pres, self.s1, self.x1, self.s2, self.a1, self.x2,
-            self.load_sem, self.out_sem, self.a_s, self.a_r, self.h_s, self.h_r,
+            self.load_sem, self.a_s, self.a_r, self.h_s, self.h_r,
             self.b_s, self.b_r, self.y_s, self.y_r,
         ) = refs
 
@@ -53,8 +53,7 @@
             plain,
             plain,
             pltpu.VMEM((n, 6 * self.half, H), BF),
-            dma((n, 2, 4)),
-            dma((n, 2, 4)),
+            dma((n, 8)),
             dma((n, 3)),
             dma((n, 3)),
             dma((n, 2)),
@@ -66,15 +65,15 @@
         ]
 
 
-SETS = ((16, FRONT + BACK), (32, BIG))
-FIELDS = 18
+SETS = ((16, FRONT + BACK), (32, max(BIG, 1)))
+FIELDS = 17
 
 
 def rows(start, size):
     return pl.ds(pl.multiple_of(start, 16), size)
 
 
-def kernel(x_hbm, bases, win_hbm, kern_hbm, wout_hbm, out_hbm, win, kern, wout, w_sem, *refs):
+def kernel(x_hbm, bases, win_hbm, kern_hbm, wout_hbm, out, win, kern, wout, w_sem, *refs):
     small = Chunks(*SETS[0], refs[:FIELDS])
     big = Chunks(*SETS[1], refs[FIELDS:])
     s = lax.axis_index("seq")
@@ -145,28 +144,21 @@
             m.y_s.at[c, 3], m.y_r.at[c, 3], partner,
         )
 
-    def moves(m, c, hbm, sem, store):
-        copies = []
+    def places(m, c):
         for h in range(2):
             if m is big:
-                there, here = hbm.at[h, pl.ds(2 * FRONT + 4 * c, 4)], m.sbuf.at[c, :, h]
-                pairs = [(there, here)]
+                yield (h, pl.ds(2 * FRONT + 4 * c, 4)), (slice(None), h)
             else:
-                first = c * 2 if c < FRONT else 2 * c + 4 * BIG
-                pairs = [
-                    (hbm.at[h, first + i // 2, pl.ds(16 * (i % 2), 16)], m.sbuf.at[c, i, h])
-                    for i in range(4)
-                ]
-            for i, (there, here) in enumerate(pairs):
-                ends = (here, there) if store else (there, here)
-                copies.append(pltpu.make_async_copy(*ends, sem.at[c, h, i]))
-        return copies
+                behind = int(c >= FRONT) if isinstance(c, int) else (c >= FRONT).astype(jnp.int32)
+                for i in range(4):
+                    group = 2 * c + 4 * BIG * behind + i // 2
+                    yield (h, group, pl.ds(16 * (i % 2), 16)), (i, h)
 
     def loads(m, c):
-        return moves(m, c, x_hbm, m.load_sem, False)
-
-    def stores(m, c):
-        return moves(m, c, out_hbm, m.out_sem, True)
+        return [
+            pltpu.make_async_copy(x_hbm.at[there], m.sbuf.at[(c, *here)], m.load_sem.at[c, i])
+            for i, (there, here) in enumerate(places(m, c))
+        ]
 
     weights = {
         "in0": pltpu.make_async_copy(win_hbm.at[0], win.at[0], w_sem.at[0]),
@@ -178,19 +170,23 @@
     }
 
     def first(m, c, *names):
-        if m is small and c == 0:
-            for name in names:
-                weights[name].wait()
+        if m is small:
+
+            @pl.when(c == 0)
+            def _():
+                for name in names:
+                    weights[name].wait()
 
     def lower_first(m, c):
         for copy in loads(m, c):
             copy.wait()
-        first(m, c, "in0")
+        if isinstance(c, int):
+            first(m, c, "in0")
         v = m.sbuf[c].reshape(m.rows, D).astype(F32)
         lowered = dot(gelu_of_norm(v), win[0])
         m.s1[c] = gelu_of_norm(lowered, m.pres[c].reshape(m.rows, 1))
-        if m is small and c == 0:
-            pl.semaphore_wait(barrier, 5 + (g + 6) // 7 + (13 - g) // 7)
+
+    def send_first(m, c):
         for k in (2, 1, 3):
             gather(m, c, k).start()
         n = 2 * m.q
@@ -247,9 +243,9 @@
         first(m, c, "out1")
         to_home(m, c).wait_recv()
         result = m.resid[c] + dot(m.a1[c], wout[1])
-        m.sbuf[c] = result.astype(BF).reshape(4, 2, m.q, D)
-        for copy in stores(m, c):
-            copy.start()
+        result = result.astype(BF).reshape(4, 2, m.q, D)
+        for there, here in places(m, c):
+            out[there] = result[here]
 
     barrier = pltpu.get_barrier_semaphore()
 
@@ -307,18 +303,43 @@
 
             return carry
 
-        lax.fori_loop(0, m.count, clear, 0)
-
-    lower_first(small, 0)
+        lax.fori_loop(0, m.count if m is small else BIG, clear, 0)
+
+    early = order[:2]
+    for m, c in early:
+        lower_first(m, c)
+    pl.semaphore_wait(barrier, 5 + (g + 6) // 7 + (13 - g) // 7)
+    for m, c in early:
+        send_first(m, c)
 
     def at(p, stage):
-        for c in range(int(stage is lower_first), FRONT + BACK):
-            pl.when(p == (c if c < FRONT else c + BIG))(lambda c=c: stage(small, c))
-        pl.when(jnp.logical_and(p >= FRONT, p < FRONT + BIG))(lambda: stage(big, p - FRONT))
+        if stage is lower_first:
+            p = p + jnp.where(p < 2, CHUNKS, 0)
+
+        def short():
+            run(small, p - BIG * (p >= FRONT).astype(jnp.int32))
+
+        def run(m, c):
+            stage(m, c)
+            if stage is lower_first:
+                send_first(m, c)
+
+        if BIG:
+            in_front = jnp.logical_and(p >= 0, p < FRONT)
+            in_back = jnp.logical_and(p >= FRONT + BIG, p < CHUNKS)
+            pl.when(jnp.logical_or(in_front, in_back))(short)
+            pl.when(jnp.logical_and(p >= FRONT, p < FRONT + BIG))(lambda: run(big, p - FRONT))
+        else:
+            pl.when(jnp.logical_and(p >= 0, p < CHUNKS))(short)
 
     PLAN = [
-        (near, 3), (pass_on, 5), (middle, 4), (far, 6),
-        (lower_first, 0), (finish, 7), (send_halo, 1),
+        (near, 3),
+        (pass_on, 5),
+        (middle, 4),
+        (far, 6),
+        (lower_first, 0),
+        (finish, 7),
+        (send_halo, 1),
     ]
 
     def step(t, carry):
@@ -337,11 +358,8 @@
             to_cross(m, c).wait_send()
             relay(m, c).wait_send()
             to_home(m, c).wait_send()
-            for copy in stores(m, c):
-                copy.wait()
-
-        for c in range(m.count):
-            drain(m, c)
+
+        lax.fori_loop(0, m.count if m is small else BIG, lambda c, carry: (drain(m, c), carry)[1], 0)
 
 
 def body(stream, bases, input_weight, kernel_weight, output_weight):
@@ -350,9 +368,9 @@
     shape = (2, PITCH // 32, 32, D)
     result = pl.pallas_call(
         kernel,
-        out_shape=jax.ShapeDtypeStruct(shape, BF),
+        out_shape=pltpu.VMEM(shape, BF),
         in_specs=[hbm, vmem, hbm, hbm, hbm],
-        out_specs=hbm,
+        out_specs=vmem,
         scratch_shapes=[
             pltpu.VMEM((2, D, H), BF),
             pltpu.VMEM((2, TAPS * H, H), BF),

time: 99.9 us -> 95.1 us (0.952)
  local copies, waits for them, and re-layouts: 4.74 us -> 2.15 us
  Pallas kernels: 94.4 us -> 92.6 us
    unnamed x1, local copies, waits for them, and re-layouts: 4.74 us -> 2.15 us
    pallas_call x1, Pallas kernels: 94.4 us -> 92.6 us  [body(): pl.pallas_call(kernel, out_shape=pltpu.VMEM(shape, BF), in_specs=[hbm, vm...]
where the time goes in v1:
time: 95.1 us; the launch traced here: 94.7 us
  Pallas kernels  92.6 us (97%)
  local copies, waits for them, and re-layouts  2.15 us (2%)
    pallas_call x1, Pallas kernels, body(): pl.pallas_call(kernel, out_shape=pltpu.VMEM(shape, BF), in_specs=[hbm, vm...  92.6 us
    unnamed x1, local copies, waits for them, and re-layouts  2.15 us

profile of v1, /device:TPU:2, one launch (start us, length us, event | category | flops | bytes accessed | tf_op | source)
XLA Modules:
  0.0 94.7 jit_solution(11853915097390263043)
XLA Ops:
  0.0 92.6 %shard_map.55 = bf16[2,28,32,1280]{3,2,1,0:T(8,128)(2,1)S(1)} custom-call(bf16[2,28,32,1280]{3,2,1,0:T(8,128)(2,1)} %bitcast.6, s32[14,128]{1,0:T(8,128)} %bitcast.7, bf16[2,1280,640]{2,1,0:T(8,128)(2,1)} %win_hbm.1, bf16[2,3200,640]{2,1,0:T(8,128)(2,1)} %bitcast.5, bf16[2,640,1280]{2,1,0:T(8,128)(2,1)} %wout_hbm.1), custom_call_target="tpu_custom_call" | custom-call | tf_op jit(solution)/shard_map/pallas_call | solution.py:369
  92.6 2.1 %copy.7 = bf16[1792,1280]{1,0:T(8,128)(2,1)} copy(bf16[1792,1280]{1,0:T(8,128)(2,1)S(1)} %bitcast.4) | data formatting | bytes 9175040

commit v2 on v1

--- a/solution.py
+++ b/solution.py
@@ -10,6 +10,7 @@
 FRONT, BIG, BACK = 1, 6, 1
 CHUNKS = FRONT + BIG + BACK
 BF, F32 = jnp.bfloat16, jnp.float32
+PARTS = 2
 VMEM_LIMIT = 54 * 2**20
 
 
@@ -32,6 +33,9 @@
     def __init__(self, q, count, refs):
         self.q, self.count = q, count
         self.rows, self.half = 8 * q, 4 * q
+        count = PARTS if q == 32 else 1
+        size = self.rows // count
+        self.parts = [slice(i * size, (i + 1) * size) for i in range(count)]
         if refs is None:
             return
         (
@@ -83,29 +87,30 @@
     own_v = low + upper - 2 * low * upper
     partner = s + 8 - 16 * low
     cross = (3 - y) * 8 + s % 8
-    base = s - z
+    batch = lax.axis_index("batch")
+    peers = [(z + k) % 4 for k in range(4)]
+    ring = [s - z + p for p in peers]
+    own_slot, partner_slot = y + 1, y + 2 - 2 * low
+    keep, give = 1 - own_v, own_v
 
     def remote(src, dst, send, recv, dev):
         return pltpu.make_async_remote_copy(
             src_ref=src, dst_ref=dst, send_sem=send, recv_sem=recv,
-            device_id={"seq": dev}, device_id_type=pl.DeviceIdType.MESH,
-        )
-
-    def peer(k):
-        return (z + k) % 4
+            device_id=(dev, batch), device_id_type=pl.DeviceIdType.MESH,
+        )
 
     def gather(m, c, k):
-        p, n = peer(k), 2 * m.q
+        p, n = peers[k], 2 * m.q
         return remote(
             m.s1.at[c, rows(p * n, n)], m.x1.at[c, rows((1 + z) * n, n)],
-            m.a_s.at[c, k - 1], m.a_r.at[c, k - 1], base + p,
+            m.a_s.at[c, k - 1], m.a_r.at[c, k - 1], ring[k],
         )
 
     def back(m, c, k):
-        p, n = peer(k), 2 * m.q
+        p, n = peers[k], 2 * m.q
         return remote(
             m.s2.at[c, rows(p * n, n)], m.a1.at[c, rows(z * n, n)],
-            m.b_s.at[c, k - 1], m.b_r.at[c, k - 1], base + p,
+            m.b_s.at[c, k - 1], m.b_r.at[c, k - 1], ring[k],
         )
 
     def halo_up(m, c):
@@ -124,23 +129,23 @@
 
     def to_partner(m, c):
         return remote(
-            m.s2.at[c, rows(own_v * m.half, m.half)], m.x2.at[c, rows((y + 1) * m.half, m.half)],
+            m.s2.at[c, rows(give * m.half, m.half)], m.x2.at[c, rows(own_slot * m.half, m.half)],
             m.y_s.at[c, 0], m.y_r.at[c, 0], partner,
         )
 
     def to_cross(m, c):
         return remote(
-            m.s2.at[c, rows((1 - own_v) * m.half, m.half)], m.x2.at[c, rows((y + 1) * m.half, m.half)],
+            m.s2.at[c, rows(keep * m.half, m.half)], m.x2.at[c, rows(own_slot * m.half, m.half)],
             m.y_s.at[c, 1], m.y_r.at[c, 1], cross,
         )
 
     def relay(m, c):
-        part = m.x2.at[c, rows((y + 2 - 2 * low) * m.half, m.half)]
+        part = m.x2.at[c, rows(partner_slot * m.half, m.half)]
         return remote(part, part, m.y_s.at[c, 2], m.y_r.at[c, 2], cross)
 
     def to_home(m, c):
         return remote(
-            m.s1.at[c, rows((1 - low) * m.half, m.half)], m.a1.at[c, rows((1 - own_v) * m.half, m.half)],
+            m.s1.at[c, rows((1 - low) * m.half, m.half)], m.a1.at[c, rows(keep * m.half, m.half)],
             m.y_s.at[c, 3], m.y_r.at[c, 3], partner,
         )
 
@@ -182,9 +187,12 @@
             copy.wait()
         if isinstance(c, int):
             first(m, c, "in0")
-        v = m.sbuf[c].reshape(m.rows, D).astype(F32)
-        lowered = dot(gelu_of_norm(v), win[0])
-        m.s1[c] = gelu_of_norm(lowered, m.pres[c].reshape(m.rows, 1))
+        mask = m.pres[c].reshape(m.rows, 1)
+        v = m.sbuf[c].reshape(m.rows, D)
+        normed = [gelu_of_norm(v[part].astype(F32)) for part in m.parts]
+        lowered = [dot(n, win[0]) for n in normed]
+        for part, low_part in zip(m.parts, lowered):
+            m.s1[c, part] = gelu_of_norm(low_part, mask[part])
 
     def send_first(m, c):
         for k in (2, 1, 3):
@@ -202,8 +210,10 @@
         first(m, c, "k0")
         pl.when(g > 0)(lambda: halo_up(m, c).wait_recv())
         pl.when(g < 7)(lambda: halo_down(m, c).wait_recv())
-        wide = jnp.concatenate([m.x1[c, pl.ds(k * m.q, 8 * m.q)] for k in range(TAPS)], axis=1)
-        m.s2[c] = gelu_of_norm(dot(wide, kern[0]))
+        for part in m.parts:
+            size = part.stop - part.start
+            wide = [m.x1[c, pl.ds(k * m.q + part.start, size)] for k in range(TAPS)]
+            m.s2[c, part] = gelu_of_norm(dot(jnp.concatenate(wide, axis=1), kern[0]))
         for k in (2, 1, 3):
             back(m, c, k).start()
         n = 2 * m.q
@@ -213,14 +223,21 @@
         first(m, c, "out0", "in1")
         for k in (1, 2, 3):
             back(m, c, k).wait_recv()
-        m.resid[c] = m.sbuf[c].reshape(m.rows, D).astype(F32) + dot(m.a1[c], wout[0])
-        lowered = dot(gelu_of_norm(m.resid[c]), win[1])
         for k in (1, 2, 3):
             back(m, c, k).wait_send()
-        m.s2[c] = gelu_of_norm(lowered, m.pres[c].reshape(m.rows, 1))
+        mask = m.pres[c].reshape(m.rows, 1)
+        v = m.sbuf[c].reshape(m.rows, D)
+        normed = []
+        for part in m.parts:
+            total = v[part].astype(F32) + dot(m.a1[c, part], wout[0])
+            m.resid[c, part] = total
+            normed.append(gelu_of_norm(total))
+        lowered = [dot(n, win[1]) for n in normed]
+        for part, low_part in zip(m.parts, lowered):
+            m.s2[c, part] = gelu_of_norm(low_part, mask[part])
         to_partner(m, c).start()
         to_cross(m, c).start()
-        m.x2[c, rows((y + 1) * m.half, m.half)] = m.s2[c, rows((1 - own_v) * m.half, m.half)]
+        m.x2[c, rows(own_slot * m.half, m.half)] = m.s2[c, rows(keep * m.half, m.half)]
 
     def pass_on(m, c):
         to_partner(m, c).wait_recv()
@@ -232,12 +249,13 @@
         relay(m, c).wait_recv()
         for k in (1, 2, 3):
             gather(m, c, k).wait_send()
-        wide = jnp.concatenate(
-            [m.x2[c, rows((upper + k) * m.half, m.rows)] for k in range(4)], axis=1
-        )
-        m.s1[c] = gelu_of_norm(dot(wide, kern[1, rows((1 - upper) * H, 4 * H)]))
+        for part in m.parts:
+            size = part.stop - part.start
+            wide = [m.x2[c, rows((upper + k) * m.half + part.start, size)] for k in range(4)]
+            wide = jnp.concatenate(wide, axis=1)
+            m.s1[c, part] = gelu_of_norm(dot(wide, kern[1, rows((1 - upper) * H, 4 * H)]))
         to_home(m, c).start()
-        m.a1[c, rows((1 - own_v) * m.half, m.half)] = m.s1[c, rows(low * m.half, m.half)]
+        m.a1[c, rows(keep * m.half, m.half)] = m.s1[c, rows(low * m.half, m.half)]
 
     def finish(m, c):
         first(m, c, "out1")
@@ -250,10 +268,10 @@
     barrier = pltpu.get_barrier_semaphore()
 
     def greet(dev):
-        pl.semaphore_signal(barrier, inc=1, device_id={"seq": dev}, device_id_type=pl.DeviceIdType.MESH)
+        pl.semaphore_signal(barrier, inc=1, device_id=(dev, batch), device_id_type=pl.DeviceIdType.MESH)
 
     for k in (1, 2, 3):
-        greet(base + peer(k))
+        greet(ring[k])
     greet(partner)
     greet(cross)
     pl.when(g < 7)(lambda: greet(s + 4))
@@ -262,18 +280,14 @@
     order = [(small, c) for c in range(FRONT)]
     order += [(big, c) for c in range(BIG)]
     order += [(small, c) for c in range(FRONT, FRONT + BACK)]
-    for i, (m, c) in enumerate(order):
-        for copy in loads(m, c):
-            copy.start()
-        if i == 0:
-            weights["in0"].start()
-        if i == 1:
-            weights["k0"].start()
-        if i == 2:
-            weights["out0"].start()
-            weights["in1"].start()
-    weights["k1"].start()
-    weights["out1"].start()
+    def fetch(some):
+        for m, c in some:
+            for copy in loads(m, c):
+                copy.start()
+
+    fetch(order[:1])
+    weights["in0"].start()
+    fetch(order[1:2])
 
     known = (bases[...] != 4).astype(F32).T
     for c, (m, i) in enumerate(order):
@@ -306,8 +320,15 @@
         lax.fori_loop(0, m.count if m is small else BIG, clear, 0)
 
     early = order[:2]
-    for m, c in early:
-        lower_first(m, c)
+    lower_first(*early[0])
+    weights["k0"].start()
+    fetch(order[2:4])
+    for name in ("out0", "in1"):
+        weights[name].start()
+    fetch(order[4:])
+    for name in ("k1", "out1"):
+        weights[name].start()
+    lower_first(*early[1])
     pl.semaphore_wait(barrier, 5 + (g + 6) // 7 + (13 - g) // 7)
     for m, c in early:
         send_first(m, c)

time: 95.1 us -> 94.6 us (level)
  no operation moved by 1% of the time
where the time goes in v2:
time: 94.6 us; the launch traced here: 94.4 us
  Pallas kernels  92.3 us (98%)
  local copies, waits for them, and re-layouts  2.15 us (2%)
    pallas_call x1, Pallas kernels, body(): pl.pallas_call(kernel, out_shape=pltpu.VMEM(shape, BF), in_specs=[hbm, vm...  92.3 us
    unnamed x1, local copies, waits for them, and re-layouts  2.15 us

profile of v2, /device:TPU:2, one launch (start us, length us, event | category | flops | bytes accessed | tf_op | source)
XLA Modules:
  0.0 94.4 jit_solution(3920578413182864177)
XLA Ops:
  0.0 92.3 %shard_map.55 = bf16[2,28,32,1280]{3,2,1,0:T(8,128)(2,1)S(1)} custom-call(bf16[2,28,32,1280]{3,2,1,0:T(8,128)(2,1)} %bitcast.6, s32[14,128]{1,0:T(8,128)} %bitcast.7, bf16[2,1280,640]{2,1,0:T(8,128)(2,1)} %win_hbm.1, bf16[2,3200,640]{2,1,0:T(8,128)(2,1)} %bitcast.5, bf16[2,640,1280]{2,1,0:T(8,128)(2,1)} %wout_hbm.1), custom_call_target="tpu_custom_call" | custom-call | tf_op jit(solution)/shard_map/pallas_call | solution.py:390
  92.3 2.1 %copy.7 = bf16[1792,1280]{1,0:T(8,128)(2,1)} copy(bf16[1792,1280]{1,0:T(8,128)(2,1)S(1)} %bitcast.4) | data formatting | bytes 9175040

commit v3 on v2

--- a/solution.py
+++ b/solution.py
@@ -225,18 +225,14 @@
             back(m, c, k).wait_recv()
         for k in (1, 2, 3):
             back(m, c, k).wait_send()
-        mask = m.pres[c].reshape(m.rows, 1)
-        v = m.sbuf[c].reshape(m.rows, D)
-        normed = []
-        for part in m.parts:
-            total = v[part].astype(F32) + dot(m.a1[c, part], wout[0])
+        for which, send in ((give, to_partner), (keep, to_cross)):
+            part, runs = rows(which * m.half, m.half), pl.ds(2 * which, 2)
+            v = m.sbuf[c, runs].reshape(m.half, D)
+            total = v.astype(F32) + dot(m.a1[c, part], wout[0])
             m.resid[c, part] = total
-            normed.append(gelu_of_norm(total))
-        lowered = [dot(n, win[1]) for n in normed]
-        for part, low_part in zip(m.parts, lowered):
-            m.s2[c, part] = gelu_of_norm(low_part, mask[part])
-        to_partner(m, c).start()
-        to_cross(m, c).start()
+            lowered = dot(gelu_of_norm(total), win[1])
+            m.s2[c, part] = gelu_of_norm(lowered, m.pres[c, runs].reshape(m.half, 1))
+            send(m, c).start()
         m.x2[c, rows(own_slot * m.half, m.half)] = m.s2[c, rows(keep * m.half, m.half)]
 
     def pass_on(m, c):

time: 94.6 us -> 95.4 us (level)
  no operation moved by 1% of the time
where the time goes in v3:
time: 95.4 us; the launch traced here: 95.2 us
  Pallas kernels  93.1 us (98%)
  local copies, waits for them, and re-layouts  2.15 us (2%)
    pallas_call x1, Pallas kernels, body(): pl.pallas_call(kernel, out_shape=pltpu.VMEM(shape, BF), in_specs=[hbm, vm...  93.1 us
    unnamed x1, local copies, waits for them, and re-layouts  2.15 us

profile of v3, /device:TPU:2, one launch (start us, length us, event | category | flops | bytes accessed | tf_op | source)
XLA Modules:
  0.0 95.2 jit_solution(806696698647067205)
XLA Ops:
  0.0 93.1 %shard_map.55 = bf16[2,28,32,1280]{3,2,1,0:T(8,128)(2,1)S(1)} custom-call(bf16[2,28,32,1280]{3,2,1,0:T(8,128)(2,1)} %bitcast.6, s32[14,128]{1,0:T(8,128)} %bitcast.7, bf16[2,1280,640]{2,1,0:T(8,128)(2,1)} %win_hbm.1, bf16[2,3200,640]{2,1,0:T(8,128)(2,1)} %bitcast.5, bf16[2,640,1280]{2,1,0:T(8,128)(2,1)} %wout_hbm.1), custom_call_target="tpu_custom_call" | custom-call | tf_op jit(solution)/shard_map/pallas_call | solution.py:386
  93.1 2.1 %copy.7 = bf16[1792,1280]{1,0:T(8,128)(2,1)} copy(bf16[1792,1280]{1,0:T(8,128)(2,1)S(1)} %bitcast.4) | data formatting | bytes 9175040

commit v4 on v2

--- a/solution.py
+++ b/solution.py
@@ -354,12 +354,12 @@
             pl.when(jnp.logical_and(p >= 0, p < CHUNKS))(short)
 
     PLAN = [
+        (finish, 8),
         (near, 3),
         (pass_on, 5),
         (middle, 4),
         (far, 6),
         (lower_first, 0),
-        (finish, 7),
         (send_halo, 1),
     ]
 

time: 94.6 us -> 94.7 us (level)
  no operation moved by 1% of the time
where the time goes in v4:
time: 94.7 us; the launch traced here: 94.5 us
  Pallas kernels  92.3 us (97%)
  local copies, waits for them, and re-layouts  2.15 us (2%)
    pallas_call x1, Pallas kernels, body(): pl.pallas_call(kernel, out_shape=pltpu.VMEM(shape, BF), in_specs=[hbm, vm...  92.3 us
    unnamed x1, local copies, waits for them, and re-layouts  2.15 us

profile of v4, /device:TPU:2, one launch (start us, length us, event | category | flops | bytes accessed | tf_op | source)
XLA Modules:
  0.0 94.5 jit_solution(2189789552379516247)
XLA Ops:
  0.0 92.3 %shard_map.55 = bf16[2,28,32,1280]{3,2,1,0:T(8,128)(2,1)S(1)} custom-call(bf16[2,28,32,1280]{3,2,1,0:T(8,128)(2,1)} %bitcast.6, s32[14,128]{1,0:T(8,128)} %bitcast.7, bf16[2,1280,640]{2,1,0:T(8,128)(2,1)} %win_hbm.1, bf16[2,3200,640]{2,1,0:T(8,128)(2,1)} %bitcast.5, bf16[2,640,1280]{2,1,0:T(8,128)(2,1)} %wout_hbm.1), custom_call_target="tpu_custom_call" | custom-call | tf_op jit(solution)/shard_map/pallas_call | solution.py:390
  92.3 2.1 %copy.7 = bf16[1792,1280]{1,0:T(8,128)(2,1)} copy(bf16[1792,1280]{1,0:T(8,128)(2,1)S(1)} %bitcast.4) | data formatting | bytes 9175040
